TPU v7x, 32 devices: a whole 2x2x4 slice. The times are simulated.
32 devices in a mesh: blk: 2 (over core), row: 16 (over z, y, x).
Axes of the slice: x: 2, y: 2, z: 4, core: 2. Of those that a mesh axis runs over, the one named last changes fastest.
Arguments:
- queries: bfloat16 [16, 16, 8192], P('row', None, 'blk')
- new_keys: bfloat16 [16, 16, 1024], P('row', None, 'blk')
- new_values: bfloat16 [16, 16, 1024], P('row', None, 'blk'), may hold values from -6 to 6
- cache_keys: bfloat16 [16, 1024, 1024], P('row', 'blk')
- cache_values: bfloat16 [16, 1024, 1024], P('row', 'blk'), may hold values from -6 to 6
- lengths: int32 [16], replicated, may hold values from 1 to 1024, as said below
- resid: bfloat16 [16, 16, 5120], P('row', 'blk'), may hold values from -6 to 6
- out_proj: bfloat16 [8192, 5120], P('blk'), may hold values from -0.0625 to 0.0625
- norm_gain: float32 [5120], replicated, may hold values from 0.1 to 1.9
- w_gate: bfloat16 [16, 5120, 3200], P('row', None, 'blk'), may hold values from -0.078125 to 0.078125
- w_up: bfloat16 [16, 5120, 3200], P('row', None, 'blk'), may hold values from -0.078125 to 0.078125
- w_down: bfloat16 [16, 3200, 5120], P('row', 'blk'), may hold values from -0.0546875 to 0.0546875
Outputs:
- attended: bfloat16 [16, 16, 5120], P('row', 'blk')
- layer_out: bfloat16 [16, 16, 5120], P('row', 'blk')
Inputs may be any that keep to these rules, and one draw needn't show every extreme that they name: `lengths`: entries of rows 12 and above are not read; some row has all 1024 positions cached.
All inputs are finite; a program needn't handle non-finite values.
Results may differ from a plain program's by a relative error of at most 0.0044.
Values may be sent and summed in bfloat16 or wider, within the bound.
A program may use at most 256 MiB of HBM per device.

v0:
```python
import math

import jax
import jax.numpy as jnp
from jax import lax
from jax.sharding import PartitionSpec as P

HEADS = 64
KV = 8
HD = 128


def from_behind(value, axis, steps):
    count = lax.axis_size(axis)
    pairs = [(source, (source + steps) % count) for source in range(count)]
    return lax.ppermute(value, axis, pairs)


def block_partial(query_block, key_block, value_block, allowed):
    scale = 1.0 / math.sqrt(query_block.shape[-1])
    scores = (
        jnp.einsum("tkgd,pkd->tkgp", query_block, key_block, preferred_element_type=jnp.float32)
        * scale
    )
    mask = allowed[:, None, None, :]
    peak = jnp.max(jnp.where(mask, scores, -1e30), axis=-1)
    weights = jnp.where(mask, jnp.exp(scores - peak[..., None]), 0.0)
    totals = jnp.sum(weights, axis=-1)
    summed = jnp.einsum(
        "tkgp,pkd->tkgd",
        weights.astype(jnp.bfloat16),
        value_block,
        preferred_element_type=jnp.float32,
    )
    safe = jnp.maximum(totals, 1.0)
    return (summed / safe[..., None], peak + jnp.log(safe))


def body(
    queries,
    new_keys,
    new_values,
    cache_keys,
    cache_values,
    lengths,
    resid,
    out_proj,
    norm_gain,
    w_gate,
    w_up,
    w_down,
):
    n_blk = lax.axis_size("blk")
    n_row = lax.axis_size("row")
    blk_index = lax.axis_index("blk")
    row_index = lax.axis_index("row")
    is_att = row_index < n_row - n_row // 4
    is_ffn = jnp.logical_not(is_att)
    length = lax.dynamic_index_in_dim(lengths, row_index, 0, keepdims=False)
    turn_len = queries.shape[1]
    kv_here = new_keys.shape[2] // HD
    group = HEADS // KV
    shard_len = cache_keys.shape[1]
    q_local = queries[0].reshape(turn_len, kv_here, group, HD)
    token_idx = jnp.arange(turn_len)
    turn_mask = token_idx[None, :] <= token_idx[:, None]
    cache_pos = blk_index * shard_len + jnp.arange(shard_len)
    cache_valid = jnp.broadcast_to((cache_pos < length)[None, :], (turn_len, shard_len))
    keys_here = cache_keys[0].reshape(shard_len, KV, HD)
    values_here = cache_values[0].reshape(shard_len, KV, HD)

    def empty_local():
        return (
            jnp.zeros((turn_len, kv_here, group, HD), jnp.float32),
            jnp.full((turn_len, kv_here, group), -1e30, jnp.float32),
        )

    def turn_work():
        return block_partial(
            q_local,
            new_keys[0].reshape(turn_len, kv_here, HD),
            new_values[0].reshape(turn_len, kv_here, HD),
            turn_mask,
        )

    out_turn, lse_turn = lax.cond(is_att, turn_work, empty_local)

    def visit(step_num, state):
        q_block, accum, run_max, run_sum = state
        source = (blk_index - step_num) % n_blk
        keys_pick = lax.dynamic_slice_in_dim(keys_here, source * kv_here, kv_here, 1)
        values_pick = lax.dynamic_slice_in_dim(values_here, source * kv_here, kv_here, 1)

        def shard_work():
            return block_partial(q_block, keys_pick, values_pick, cache_valid)

        out_blk, lse_blk = lax.cond(is_att, shard_work, empty_local)
        new_max = jnp.maximum(run_max, lse_blk)
        fading = jnp.exp(run_max - new_max)
        lifting = jnp.exp(lse_blk - new_max)
        accum = accum * fading[..., None] + out_blk * lifting[..., None]
        run_sum = run_sum * fading + lifting
        q_block = from_behind(q_block, "blk", 1)
        accum, new_max, run_sum = from_behind((accum, new_max, run_sum), "blk", 1)
        return (q_block, accum, new_max, run_sum)

    start_state = (q_local, out_turn, lse_turn, jnp.ones_like(lse_turn))
    final_state = lax.fori_loop(0, n_blk, visit, start_state)
    accum = final_state[1]
    run_sum = final_state[3]
    attn_rows = (
        (accum / run_sum[..., None]).reshape(turn_len, kv_here * group * HD).astype(jnp.bfloat16)
    )
    rows_here = resid.shape[1]
    width = out_proj.shape[1]

    def proj_work():
        return jnp.dot(attn_rows, out_proj, preferred_element_type=jnp.float32)

    projected = lax.psum_scatter(
        lax.cond(
            is_att,
            proj_work,
            lambda: jnp.zeros((rows_here * lax.axis_size("blk"), width), jnp.float32),
        ),
        "blk",
        scatter_dimension=0,
        tiled=True,
    )
    mid = resid[0].astype(jnp.float32) + projected
    normed = (
        mid * lax.rsqrt(jnp.mean(mid * mid, axis=-1, keepdims=True) + 1e-06) * norm_gain
    ).astype(jnp.bfloat16)
    gate_slab = w_gate[0]
    up_slab = w_up[0]
    down_slab = w_down[0]
    row_tokens = lax.all_gather(normed, "row", axis=0, tiled=True)
    tokens_in = lax.all_gather(row_tokens, "blk", axis=0, tiled=True)

    def ffn_work():
        gate = jnp.dot(tokens_in, gate_slab, preferred_element_type=jnp.float32)
        upper = jnp.dot(tokens_in, up_slab, preferred_element_type=jnp.float32)
        return (jax.nn.silu(gate) * upper).astype(jnp.bfloat16)

    hidden = lax.cond(
        is_ffn, ffn_work, lambda: jnp.zeros((tokens_in.shape[0], gate_slab.shape[1]), jnp.bfloat16)
    )

    def down_work():
        return jnp.dot(hidden, down_slab, preferred_element_type=jnp.float32)

    slab_sums = lax.psum_scatter(
        lax.cond(
            is_ffn,
            down_work,
            lambda: jnp.zeros((rows_here * n_row * lax.axis_size("blk"), width), jnp.float32),
        ),
        "blk",
        scatter_dimension=0,
        tiled=True,
    )
    ffn = lax.psum_scatter(slab_sums, "row", scatter_dimension=0, tiled=True)
    attended = jnp.where(is_att, mid, 0.0).astype(jnp.bfloat16)[None]
    layer_out = jnp.where(is_att, mid + ffn, 0.0).astype(jnp.bfloat16)[None]
    return (attended, layer_out)


def solution(mesh):
    placed = (
        P("row", None, "blk"),
        P("row", None, "blk"),
        P("row", None, "blk"),
        P("row", "blk", None),
        P("row", "blk", None),
        P(),
        P("row", "blk", None),
        P("blk", None),
        P(),
        P("row", None, "blk"),
        P("row", None, "blk"),
        P("row", "blk", None),
    )
    return jax.shard_map(
        body,
        mesh=mesh,
        in_specs=placed,
        out_specs=(P("row", "blk", None), P("row", "blk", None)),
        check_vma=False,
    )
```

profile of v0, /device:TPU:0, one launch (start us, length us, event | category | flops | bytes accessed | tf_op | source)
XLA Modules:
  0.0 259.5 jit_solution(10340998323897789768)
XLA Ops:
  7.3 1.0 copy.64
  8.3 1.5 copy.43
  9.8 0.7 copy.46
  11.7 0.7 dynamic_slice.36
  12.4 0.7 add_compare_fusion
  13.2 1.0 conditional.5
  14.2 7.6 %while.22 = (s32[]{:T(128)}, bf16[16,4,8,128]{3,0,2,1:T(8,128)(2,1)S(1)}, f32[16,4,8,128]{3,2,0,1:T(8,128)S(1)}, f32[16,4,8]{0,2,1:T(8,128)S(1)}, f32[16,4,8]{0,...) while((s32[]{:T(128)}, ...), condition=%wide.region_9.10_spmd.clone, body=%wide.region_4.9_spmd.clone.sunk | while | flops 136317456 | bytes 7304721 | solution.py:108
  14.2 1.3 conditional.11
  17.0 0.8 collective-permute-done.2
  18.2 1.3 conditional.11
  21.0 0.7 collective-permute-done.2
  21.8 16.0 %conditional.6 = (f32[16,5120]{1,0:T(8,128)S(1)}) conditional(s32[]{:T(128)} %convert_element_type.56, () %tuple.86, (f32[16,4,8]{0,2,1:T(8,128)S(1)}, f32[16,4,8,128]{3,2,0,1:T(8,128)S(1)}, bf16[4096,5120]{1,0:T(8,128)(2,1)}) %tuple.90), branch_computations={%region_10.11_spmd, %region_11.12_spmd} | conditional | flops 671219712 | bytes 42801160 | solution.py:121
  22.1 15.7 %fusion.10 = f32[16,5120]{1,0:T(8,128)S(1)} fusion(bf16[4096,5120]{1,0:T(8,128)(2,1)} %get-tuple-element.443, bf16[2,8,32,128]{3,2,1,0:T(8,128)(2,1)S(1)} %bitcast.82), kind=kOutput, calls=%fused_computation.16 | convolution fusion | flops 671088640 | bytes 42401792 | tf_op jit(solution)/shard_map/cond/branch_1_fun/dot_general | solution.py:118
  37.8 0.7 copy-done.1
  38.6 9.4 %reduce-scatter.4.cloned.1.call-done = f32[8,5120]{1,0:T(8,128)} async-done(((f32[16,5120]{1,0:T(8,128)}), f32[8,5120]{1,0:T(8,128)}) %reduce-scatter.4.cloned.1.call-update) | async-done | bytes 163856 | tf_op jit(solution)/shard_map/reduce_scatter | solution.py:120
  48.0 1.1 multiply_reduce_fusion
  49.1 1.6 multiply_convert_fusion
  50.8 58.9 %all-gather.3.cloned.1.call-done = bf16[128,5120]{1,0:T(8,128)(2,1)} async-done(((bf16[8,5120]{1,0:T(8,128)(2,1)}), bf16[128,5120]{1,0:T(8,128)(2,1)}) %all-gather.3.cloned.1.call-update) | async-done | bytes 1310736 | tf_op jit(solution)/shard_map/all_gather | solution.py:137
  109.9 11.8 %all-gather.5.cloned.1.call-done = bf16[256,5120]{1,0:T(8,128)(2,1)} async-done(((bf16[128,5120]{1,0:T(8,128)(2,1)}), bf16[256,5120]{1,0:T(8,128)(2,1)}) %all-gather.5.cloned.1.call-update) | async-done | bytes 2621456 | tf_op jit(solution)/shard_map/all_gather | solution.py:138
  121.9 3.0 %conditional.8 = (f32[256,5120]{1,0:T(8,128)}) conditional(s32[]{:T(128)} %convert_element_type.58, () %tuple.91, (bf16[1,1600,5120]{2,1,0:T(8,128)(2,1)}, bf16[256,1600]{0,1:T(8,128)(2,1)S(1)}) %tuple.94), branch_computations={%region_16.17_spmd, %region_17.18_spmd} | conditional | flops 4194304000 | bytes 22446088 | solution.py:153
  121.9 3.0 %broadcast.92 = f32[256,5120]{1,0:T(8,128)} broadcast(f32[]{:T(128)} %constant.159.clone), dimensions={} | broadcast | bytes 5242884 | tf_op jit(solution)/shard_map/broadcast.26
  125.0 40.7 %reduce-scatter.6.cloned.1.call-done = f32[128,5120]{1,0:T(8,128)} async-done(((f32[256,5120]{1,0:T(8,128)}), f32[128,5120]{1,0:T(8,128)}) %reduce-scatter.6.cloned.1.call-update) | async-done | bytes 2621456 | tf_op jit(solution)/shard_map/reduce_scatter | solution.py:152
  165.7 85.6 %reduce-scatter.8.cloned.1.call-done = f32[8,5120]{1,0:T(8,128)} async-done(((f32[128,5120]{1,0:T(8,128)}), f32[8,5120]{1,0:T(8,128)}) %reduce-scatter.8.cloned.1.call-update) | async-done | bytes 163856 | tf_op jit(solution)/shard_map/reduce_scatter | solution.py:162
  251.3 1.6 fusion.37
  (79 shorter events, 9.0 us)
Async XLA Ops:
  7.2 3.3 %copy-start.2 = (bf16[1,512,1024]{2,1,0:T(8,128)(2,1)S(1)}, bf16[1,512,1024]{2,1,0:T(8,128)(2,1)}, u32[]{:S(2)}) copy-start(bf16[1,512,1024]{2,1,0:T(8,128)(2,1)} %param.28) | copy-start | bytes 3145732
  7.2 4.6 %copy-start.9 = (s32[16]{0:T(128)S(1)}, s32[16]{0:T(128)}, u32[]{:S(2)}) copy-start(s32[16]{0:T(128)} %param.29) | copy-start | bytes 196
  7.2 5.9 %copy-start.6 = (bf16[1,16,512]{2,1,0:T(8,128)(2,1)S(1)}, bf16[1,16,512]{2,1,0:T(8,128)(2,1)}, u32[]{:S(2)}) copy-start(bf16[1,16,512]{2,1,0:T(8,128)(2,1)} %param.26) | copy-start | bytes 49156
  7.2 5.9 %copy-start.5 = (bf16[1,16,512]{2,1,0:T(8,128)(2,1)S(1)}, bf16[1,16,512]{2,1,0:T(8,128)(2,1)}, u32[]{:S(2)}) copy-start(bf16[1,16,512]{2,1,0:T(8,128)(2,1)} %param.25) | copy-start | bytes 49156
  7.2 40.8 %reduce-scatter.4.cloned.1.call-start = ((), (), s32[]{:S(2)}) async-start(), calls=%async_computation.3 | async-start | bytes 491520 | tf_op jit(solution)/shard_map/reduce_scatter | solution.py:120
  15.9 2.2 collective-permute-start.1
  16.5 1.7 collective-permute-start
  16.5 1.3 collective-permute-start.2
  17.0 1.2 collective-permute-start.3
  19.9 1.9 collective-permute-start.1
  20.1 1.7 collective-permute-start
  20.5 1.2 collective-permute-start.2
  20.6 1.2 collective-permute-start.3
  21.8 26.2 %copy-start.3 = (bf16[1,8,5120]{2,1,0:T(8,128)(2,1)S(1)}, bf16[1,8,5120]{2,1,0:T(8,128)(2,1)}, u32[]{:S(2)}) copy-start(bf16[1,8,5120]{2,1,0:T(8,128)(2,1)} %param.30) | copy-start | bytes 245764
  21.8 27.3 %copy-start.4 = (f32[5120]{0:T(1024)S(1)}, f32[5120]{0:T(1024)}, u32[]{:S(2)}) copy-start(f32[5120]{0:T(1024)} %param.32) | copy-start | bytes 61444
  37.8 0.7 copy-start.1
  38.6 71.2 %all-gather.3.cloned.1.call-start = ((), (), s32[]{:S(2)}) async-start(), calls=%async_computation.4 | async-start | bytes 1392640 | tf_op jit(solution)/shard_map/all_gather | solution.py:137
  50.8 70.9 %all-gather.5.cloned.1.call-start = ((), (), s32[]{:S(2)}) async-start(), calls=%async_computation.5 | async-start | bytes 3932160 | tf_op jit(solution)/shard_map/all_gather | solution.py:138
  109.8 55.9 %reduce-scatter.6.cloned.1.call-start = ((), (), s32[]{:S(2)}) async-start(), calls=%async_computation.6 | async-start | bytes 7864320 | tf_op jit(solution)/shard_map/reduce_scatter | solution.py:152
  124.9 126.4 %copy-start = (f32[8,5120]{1,0:T(8,128)S(1)}, f32[8,5120]{1,0:T(8,128)}, u32[]{:S(2)}) copy-start(f32[8,5120]{1,0:T(8,128)} %reduce-scatter.4.cloned.1.call-done) | copy-start | bytes 491524
  124.9 126.4 %reduce-scatter.8.cloned.1.call-start = ((), (), s32[]{:S(2)}) async-start(), calls=%async_computation.7 | async-start | bytes 2785280 | tf_op jit(solution)/shard_map/reduce_scatter | solution.py:162
Sparse Core Ops, SparseCore 0:
  38.7 9.2 reduce-scatter.3
  51.7 58.0 all-gather.2
  111.4 10.2 all-gather.4
  125.1 40.5 reduce-scatter.5
  167.8 83.4 reduce-scatter.7
where the time goes:
time: 260 us; the launch traced here: 259 us
  waiting for transfers between devices  208 us (80%)
  matrix products  18 us (7%)
  between operations  14 us (5%)
  local copies, waits for them, and re-layouts  9.67 us (4%)
  other arithmetic  6.44 us (2%)
    reduce_scatter x1, waiting for transfers between devices, body(): ffn = lax.psum_scatter(slab_sums, 'row', scatter_dimension=0, tiled=True)  85.6 us
    all_gather x1, waiting for transfers between devices, body(): row_tokens = lax.all_gather(normed, 'row', axis=0, tiled=True)  58.9 us
    reduce_scatter x1, waiting for transfers between devices, body(): lax.psum_scatter(lax.cond(is_ffn, down_work, lambda: jnp.zeros((rows_here...  40.7 us
    dot_general x1, matrix products, proj_work(): return jnp.dot(attn_rows, out_proj, preferred_element_type=jnp.float32)  15.7 us
    all_gather x1, waiting for transfers between devices, body(): tokens_in = lax.all_gather(row_tokens, 'blk', axis=0, tiled=True)  11.8 us
    reduce_scatter x1, waiting for transfers between devices, body(): lax.psum_scatter(lax.cond(is_att, proj_work, lambda: jnp.zeros((rows_here...  9.39 us
  transfers between devices with their start and end apart: 13, of which 9 were waited for; matrix products, arithmetic and copies ran while one was open for 0% of the time, Pallas kernels for 0%

commit v1 on v0

v1 whole, which is shorter than its diff:
```python
import functools
import math

import jax
import jax.numpy as jnp
from jax import lax
from jax.experimental import pallas as pl
from jax.experimental.pallas import tpu as pltpu
from jax.sharding import PartitionSpec as P

HD = 128
GROUP = 8
MESH = pl.DeviceIdType.MESH
F32 = jnp.float32
BF16 = jnp.bfloat16
TILE = 256
SPAN = 512
DEPTH = 512


def contract_last(a, b):
    return lax.dot_general(a, b, (((1,), (1,)), ((), ())), preferred_element_type=F32)


def kernel(
    n_row, n_slot,
    lengths, queries, new_keys, new_values, cache_keys, cache_values, resid, out_proj, gain,
    w_gate, w_up, w_down,
    attended, layer_out,
    k_far, v_far, acc, acc_far, normed, tokens, ffn_in,
    core_out, core_in, plane_out, plane_in, final,
    kv_send, kv_recv, acc_sems, norm_send, tok_recv, tok_send, relay_send, relay_recv,
    core_send, core_recv, plane_send, plane_recv, final_send, ffn_recv, mate_send, mate_recv,
):
    blk = lax.axis_index("blk")
    row = lax.axis_index("row")
    mate = 1 - blk
    n_ffn = n_row // 4
    n_att = n_row - n_ffn
    per = n_att // n_ffn
    turn = queries.shape[1]
    width = out_proj.shape[1]
    half = width // 2
    n_piece = half // SPAN
    local = new_keys.shape[2]
    kv_here = local // HD
    shard = cache_keys.shape[1]
    n_chunk = out_proj.shape[0] // DEPTH
    units = w_gate.shape[1]
    sibling = {"blk": mate, "row": row}
    my_cols = pl.ds(pl.multiple_of(blk * half, 128), half)
    mate_cols = pl.ds(pl.multiple_of(mate * half, 128), half)
    barrier = pltpu.get_barrier_semaphore()

    def remote(src, dst, send, recv, device):
        return pltpu.make_async_remote_copy(
            src_ref=src, dst_ref=dst, send_sem=send, recv_sem=recv,
            device_id=device, device_id_type=MESH,
        )

    def greet(device):
        pl.semaphore_signal(barrier, inc=1, device_id=device, device_id_type=MESH)

    def attention(wo_buf, k_own, v_own, attn, mid, wo_sem, own_sem):
        column = lax.rem(row, n_ffn)
        place = lax.div(row, n_ffn)
        server = {"blk": blk, "row": n_att + column}
        greet(sibling)
        greet(server)
        own_heads = pl.ds(pl.multiple_of(blk * local, 128), local)
        far_heads = pl.ds(pl.multiple_of(mate * local, 128), local)
        own_k = pltpu.make_async_copy(cache_keys.at[0, :, own_heads], k_own, own_sem.at[0])
        own_v = pltpu.make_async_copy(cache_values.at[0, :, own_heads], v_own, own_sem.at[1])
        own_k.start()
        own_v.start()

        def wo_copy(s):
            slot = lax.rem(s, n_slot)
            return pltpu.make_async_copy(
                out_proj.at[pl.ds(pl.multiple_of(s * DEPTH, DEPTH), DEPTH)],
                wo_buf.at[slot], wo_sem.at[slot],
            )

        pl.semaphore_wait(barrier, 2)
        send_k = remote(
            cache_keys.at[0, :, far_heads], k_far, kv_send.at[0], kv_recv.at[0], sibling
        )
        send_v = remote(
            cache_values.at[0, :, far_heads], v_far, kv_send.at[1], kv_recv.at[1], sibling
        )
        send_k.start()
        send_v.start()

        @pl.loop(0, min(n_slot, n_chunk))
        def _(s):
            wo_copy(s).start()

        own_k.wait()
        own_v.wait()
        send_k.wait()
        send_v.wait()

        length = lengths[row]
        scale = 1.0 / math.sqrt(HD)
        rows = turn * GROUP
        turn_mask = lax.broadcasted_iota(jnp.int32, (rows, turn), 1) <= jnp.bitwise_and(
            lax.broadcasted_iota(jnp.int32, (rows, turn), 0), turn - 1
        )
        spot = lax.broadcasted_iota(jnp.int32, (rows, shard), 1)
        own_mask = spot + blk * shard < length
        far_mask = spot + mate * shard < length
        for k in range(kv_here):
            heads = slice(k * HD, (k + 1) * HD)
            query = jnp.concatenate(
                [queries[0, :, (k * GROUP + g) * HD : (k * GROUP + g + 1) * HD]
                 for g in range(GROUP)], axis=0,
            )
            parts = []
            for mask, keys in (
                (turn_mask, new_keys[0, :, heads]),
                (own_mask, k_own[:, heads]),
                (far_mask, k_far[:, heads]),
            ):
                parts.append(jnp.where(mask, contract_last(query, keys) * scale, -1e30))
            peak = functools.reduce(
                jnp.maximum, [jnp.max(s, axis=-1, keepdims=True) for s in parts]
            )
            total = jnp.zeros((rows, 1), F32)
            summed = jnp.zeros((rows, HD), F32)
            for s, mask, values in (
                (parts[0], turn_mask, new_values[0, :, heads]),
                (parts[1], own_mask, v_own[:, heads]),
                (parts[2], far_mask, v_far[:, heads]),
            ):
                weights = jnp.where(mask, jnp.exp(s - peak), 0.0)
                total += jnp.sum(weights, axis=-1, keepdims=True)
                summed += jnp.dot(weights.astype(BF16), values, preferred_element_type=F32)
            out = (summed / total).astype(BF16)
            for g in range(GROUP):
                attn[:, (k * GROUP + g) * HD : (k * GROUP + g + 1) * HD] = out[
                    g * turn : (g + 1) * turn
                ]

        acc[...] = jnp.zeros_like(acc)
        mine = pl.ds(pl.multiple_of(blk * (turn // 2), turn // 2), turn // 2)
        acc[mine, :] = resid[0].astype(F32)

        @pl.loop(0, n_chunk)
        def _(s):
            wo_copy(s).wait()
            some = attn[:, pl.ds(pl.multiple_of(s * DEPTH, DEPTH), DEPTH)]
            acc[...] += jnp.dot(some, wo_buf[lax.rem(s, n_slot)], preferred_element_type=F32)
            if n_slot < n_chunk:
                @pl.when(s + n_slot < n_chunk)
                def _():
                    wo_copy(s + n_slot).start()

        swap = remote(acc, acc_far, acc_sems.at[0], acc_sems.at[1], sibling)
        swap.start()
        swap.wait()
        value = acc[...] + acc_far[...]
        mid[...] = value
        square = jnp.mean(value * value, axis=-1, keepdims=True)
        normed[...] = (value * lax.rsqrt(square + 1e-06) * gain[...]).astype(BF16)
        spread = remote(
            normed.at[:, my_cols],
            tokens.at[pl.ds(pl.multiple_of((column * per + place) * turn, turn), turn), my_cols],
            norm_send, tok_recv.at[column * per + place], server,
        )
        spread.start()
        attended[0] = mid[mine, :].astype(BF16)

        def mate_copy(j, side):
            cols = pl.ds(pl.multiple_of(side * half + j * SPAN, 128), SPAN)
            return remote(
                ffn_in.at[:, cols], ffn_in.at[:, cols], mate_send.at[j], mate_recv.at[j], sibling
            )

        @pl.loop(0, n_piece)
        def _(j):
            cols = pl.ds(pl.multiple_of(blk * half + j * SPAN, 128), SPAN)
            remote(
                ffn_in.at[:, cols], ffn_in.at[:, cols], mate_send.at[j], ffn_recv.at[j], sibling
            ).wait_recv()
            mate_copy(j, blk).start()

        @pl.loop(0, n_piece)
        def _(j):
            mate_copy(j, mate).wait_recv()

        @pl.loop(0, n_piece)
        def _(j):
            mate_copy(j, blk).wait_send()

        acc_far[...] = ffn_in[...].astype(F32)
        layer_out[0] = (mid[mine, :] + acc_far[mine, :]).astype(BF16)
        spread.wait_send()

    def feed_forward(gate_buf, up_buf, down_buf, hidden, w_sem):
        me = row - n_att

        gate_copy = pltpu.make_async_copy(w_gate.at[0], gate_buf, w_sem.at[0])
        up_copy = pltpu.make_async_copy(w_up.at[0], up_buf, w_sem.at[1])
        down_copy = pltpu.make_async_copy(w_down.at[0], down_buf, w_sem.at[2])
        gate_copy.start()
        up_copy.start()
        down_copy.start()
        greet(sibling)
        for i in range(per):
            greet({"blk": blk, "row": me + i * n_ffn})

        def peer(step):
            return lax.rem(me + step, n_ffn)

        def at(c):
            return {"blk": blk, "row": n_att + c}

        @pl.loop(1, n_ffn)
        def _(step):
            greet(at(peer(step)))

        pl.semaphore_wait(barrier, per + n_ffn)
        attended[...] = jnp.zeros_like(attended)
        layer_out[...] = jnp.zeros_like(layer_out)

        def piece(p, cols):
            return tokens.at[pl.ds(pl.multiple_of(p * turn, turn), turn), cols]

        def forward(i, step):
            p = me * per + i
            return remote(
                piece(p, my_cols), piece(p, my_cols), tok_send.at[i, step], tok_recv.at[p],
                at(peer(step)),
            )

        def arrive(p):
            remote(
                piece(p, my_cols), piece(p, my_cols), relay_send.at[p], tok_recv.at[p], sibling
            ).wait_recv()

        def relay(p, cols):
            return remote(
                piece(p, cols), piece(p, cols), relay_send.at[p], relay_recv.at[p], sibling
            )

        for i in reversed(range(per)):
            arrive(me * per + i)

            @pl.loop(1, n_ffn)
            def _(step):
                forward(i, step).start()

            relay(me * per + i, my_cols).start()

        for i in reversed(range(per)):
            @pl.loop(1, n_ffn)
            def _(step):
                p = peer(step) * per + i
                arrive(p)
                relay(p, my_cols).start()

        @pl.loop(0, n_att)
        def _(p):
            relay(p, mate_cols).wait_recv()

        gate_copy.wait()
        up_copy.wait()

        def block(cols):
            x = tokens[...]
            g = contract_last(x, gate_buf[cols, :])
            u = contract_last(x, up_buf[cols, :])
            hidden[:, cols] = (g / (1.0 + jnp.exp(-g)) * u).astype(BF16)

        @pl.loop(0, units // TILE)
        def _(j):
            block(pl.ds(pl.multiple_of(j * TILE, TILE), TILE))

        if units % TILE:
            block(slice(units // TILE * TILE, units))

        down_copy.wait()

        def down(side, j):
            cols = pl.ds(pl.multiple_of(side * half + j * SPAN, 128), SPAN)
            return jnp.dot(hidden[...], down_buf[:, cols], preferred_element_type=F32)

        def core_copy(j):
            return remote(core_out.at[j], core_in.at[j], core_send.at[j], core_recv.at[j], sibling)

        @pl.loop(0, n_piece)
        def _(j):
            core_out[j] = down(mate, j).astype(BF16)
            core_copy(j).start()

        def group_rows(c):
            return pl.ds(pl.multiple_of(c * per * turn, turn), per * turn)

        def plane_copy(j, step):
            c = peer(step)
            return remote(
                plane_out.at[j, group_rows(c)], plane_in.at[me, j],
                plane_send.at[j, step], plane_recv.at[me, j], at(c),
            )

        @pl.loop(0, n_piece)
        def _(j):
            part = down(blk, j)
            core_copy(j).wait_recv()
            plane_out[j] = (part + core_in[j].astype(F32)).astype(BF16)

            @pl.loop(1, n_ffn)
            def _(step):
                plane_copy(j, step).start()

        def final_copy(j, i):
            cols = pl.ds(pl.multiple_of(blk * half + j * SPAN, 128), SPAN)
            return remote(
                final.at[j, pl.ds(i * turn, turn)], ffn_in.at[:, cols],
                final_send.at[j, i], ffn_recv.at[j], {"blk": blk, "row": me + i * n_ffn},
            )

        @pl.loop(0, n_piece)
        def _(j):
            def add(step, total):
                c = peer(step)
                remote(
                    plane_out.at[j, group_rows(c)], plane_in.at[c, j],
                    plane_send.at[j, step], plane_recv.at[c, j], at(c),
                ).wait_recv()
                return total + plane_in[c, j].astype(F32)

            total = plane_out[j, group_rows(me)].astype(F32)
            final[j] = lax.fori_loop(1, n_ffn, add, total).astype(BF16)
            for i in range(per):
                final_copy(j, i).start()

        @pl.loop(0, n_piece)
        def _(j):
            core_copy(j).wait_send()
            for i in range(per):
                final_copy(j, i).wait_send()

            @pl.loop(1, n_ffn)
            def _(step):
                plane_copy(j, step).wait_send()

        for i in range(per):
            @pl.loop(1, n_ffn)
            def _(step):
                forward(i, step).wait_send()

        @pl.loop(0, n_att)
        def _(p):
            relay(p, my_cols).wait_send()

    @pl.when(row < n_att)
    def _():
        pl.run_scoped(
            attention,
            pltpu.VMEM((n_slot, DEPTH, width), BF16),
            pltpu.VMEM((shard, local), BF16),
            pltpu.VMEM((shard, local), BF16),
            pltpu.VMEM((turn, out_proj.shape[0]), BF16),
            pltpu.VMEM((turn, width), F32),
            pltpu.SemaphoreType.DMA((n_slot,)),
            pltpu.SemaphoreType.DMA((2,)),
        )

    @pl.when(row >= n_att)
    def _():
        pl.run_scoped(
            feed_forward,
            pltpu.VMEM((units, width), BF16),
            pltpu.VMEM((units, width), BF16),
            pltpu.VMEM((units, width), BF16),
            pltpu.VMEM((n_att * turn, units), BF16),
            pltpu.SemaphoreType.DMA((3,)),
        )


def body(
    queries, new_keys, new_values, cache_keys, cache_values, lengths, resid, out_proj, norm_gain,
    w_gate, w_up, w_down,
):
    n_row = lax.axis_size("row")
    n_ffn = n_row // 4
    n_att = n_row - n_ffn
    per = n_att // n_ffn
    turn = queries.shape[1]
    width = out_proj.shape[1]
    half = width // 2
    n_piece = half // SPAN
    shard = cache_keys.shape[1]
    local = new_keys.shape[2]
    n_tok = n_att * turn
    n_slot = 8 if n_tok <= 256 else 4
    vmem = pl.BlockSpec(memory_space=pltpu.VMEM)
    anywhere = pl.BlockSpec(memory_space=pl.ANY)
    dma = pltpu.SemaphoreType.DMA
    out = jax.ShapeDtypeStruct(resid.shape, BF16)
    return pl.pallas_call(
        functools.partial(kernel, n_row, n_slot),
        out_shape=(out, out),
        in_specs=[
            pl.BlockSpec(memory_space=pltpu.SMEM), vmem, vmem, vmem, anywhere, anywhere, vmem,
            anywhere, vmem, anywhere, anywhere, anywhere,
        ],
        out_specs=(vmem, vmem),
        scratch_shapes=[
            pltpu.VMEM((shard, local), BF16),
            pltpu.VMEM((shard, local), BF16),
            pltpu.VMEM((turn, width), F32),
            pltpu.VMEM((turn, width), F32),
            pltpu.VMEM((turn, width), BF16),
            pltpu.VMEM((n_tok, width), BF16),
            pltpu.VMEM((turn, width), BF16),
            pltpu.VMEM((n_piece, n_tok, SPAN), BF16),
            pltpu.VMEM((n_piece, n_tok, SPAN), BF16),
            pltpu.VMEM((n_piece, n_tok, SPAN), BF16),
            pltpu.VMEM((n_ffn, n_piece, per * turn, SPAN), BF16),
            pltpu.VMEM((n_piece, per * turn, SPAN), BF16),
            dma((2,)),
            dma((2,)),
            dma((2,)),
            dma,
            dma((n_att,)),
            dma((per, n_ffn)),
            dma((n_att,)),
            dma((n_att,)),
            dma((n_piece,)),
            dma((n_piece,)),
            dma((n_piece, n_ffn)),
            dma((n_ffn, n_piece)),
            dma((n_piece, per)),
            dma((n_piece,)),
            dma((n_piece,)),
            dma((n_piece,)),
        ],
        compiler_params=pltpu.CompilerParams(
            collective_id=0, has_side_effects=True, vmem_limit_bytes=60 * 1024 * 1024,
        ),
        cost_estimate=pl.CostEstimate(
            flops=10_000_000_000, bytes_accessed=60_000_000, transcendentals=600_000
        ),
    )(
        lengths, queries, new_keys, new_values, cache_keys, cache_values, resid, out_proj,
        norm_gain.reshape(1, width), jnp.swapaxes(w_gate, 1, 2), jnp.swapaxes(w_up, 1, 2), w_down,
    )


def solution(mesh):
    placed = (
        P("row", None, "blk"),
        P("row", None, "blk"),
        P("row", None, "blk"),
        P("row", "blk", None),
        P("row", "blk", None),
        P(),
        P("row", "blk", None),
        P("blk", None),
        P(),
        P("row", None, "blk"),
        P("row", None, "blk"),
        P("row", "blk", None),
    )
    return jax.shard_map(
        body,
        mesh=mesh,
        in_specs=placed,
        out_specs=(P("row", "blk", None), P("row", "blk", None)),
        check_vma=False,
    )
```

time: 260 us -> 80.2 us (0.31)
  waiting for transfers between devices: 208 us -> 0 us
  Pallas kernels: 0 us -> 76.3 us
  matrix products: 18 us -> 0 us
  between operations: 14 us -> 0.64 us
  local copies, waits for them, and re-layouts: 9.67 us -> 3.05 us
  other arithmetic: 6.44 us -> 0 us
    reduce_scatter x3 -> x0, waiting for transfers between devices: 136 us -> none  [the longest x1 85.6 us: body(): ffn = lax.psum_scatter(slab_sums, 'row', scatter_dimension=0, tiled=True)]
    pallas_call x0 -> x1, Pallas kernels: none -> 76.3 us  [body(): pl.pallas_call(functools.partial(kernel, n_row, n_slot), out_shape=(out,...]
    all_gather x2 -> x0, waiting for transfers between devices: 70.8 us -> none  [the longest x1 58.9 us: body(): row_tokens = lax.all_gather(normed, 'row', axis=0, tiled=True)]
    dot_general x7 -> x0, matrix products: 18 us -> none  [the longest x1 15.7 us: proj_work(): return jnp.dot(attn_rows, out_proj, preferred_element_type=jnp.float32)]
    another operation x4 -> x0, local copies, waits for them, and re-layouts: 3.1 us -> none
  transfers between devices with their start and end apart: 13 -> 0, of which waited for: 9 -> 0; matrix products, arithmetic and copies ran while one was open for 0% -> 0% of each run, Pallas kernels for 0% -> 0%
where the time goes in v1:
time: 80.2 us; the launch traced here: 80 us
  Pallas kernels  76.3 us (95%)
  local copies, waits for them, and re-layouts  3.05 us (4%)
    pallas_call x1, Pallas kernels, body(): pl.pallas_call(functools.partial(kernel, n_row, n_slot), out_shape=(out,...  76.3 us
    unnamed x2, local copies, waits for them, and re-layouts  3.05 us

profile of v1, /device:TPU:0, one launch (start us, length us, event | category | flops | bytes accessed | tf_op | source)
XLA Modules:
  0.0 80.0 jit_solution(7726986076509526198)
XLA Ops:
  0.6 76.3 %shard_map.131 = (bf16[1,8,5120]{2,1,0:T(8,128)(2,1)}, bf16[1,8,5120]{2,1,0:T(8,128)(2,1)}) custom-call(s32[16]{0:T(128)} %lengths.1, bf16[1,16,4096]{2,1,0:T(8,128)(2,1)} %queries.1, bf16[1,16,512]{2,1,0:T(8,128)(2,1)} %new_keys.1, bf16[1,16,512]{2,1,0:T(8,128)(2,1)} %new_values.1, bf16[1,512,1024]{2,1,0:T(8,128)(2,1)} %cache_keys.1, ...), custom_call_target="tpu_custom_call" | custom-call | flops 10000000000 | bytes 60000000 | tf_op jit(solution)/shard_map/pallas_call | solution.py:402
  76.9 1.5 %copy.16 = bf16[1,8,5120]{2,1,0:T(8,128)(2,1)} copy(bf16[1,8,5120]{2,1,0:T(8,128)(2,1)} %get-tuple-element.4) | data formatting | bytes 163840
  78.5 1.5 %copy.17 = bf16[1,8,5120]{2,1,0:T(8,128)(2,1)} copy(bf16[1,8,5120]{2,1,0:T(8,128)(2,1)} %get-tuple-element.5) | data formatting | bytes 163840
